TPU v7x, 512 devices: a whole 4x4x16 slice. The times are simulated.
512 devices in a mesh: chan: 4 (over y), row: 16 (over x, z_hi), col: 8 (over z_lo, core).
Axes of the slice: x: 4, y: 4, z: 16 (z_hi: 4, z_lo: 4; z = z_hi * 4 + z_lo), core: 2. Of those that a mesh axis runs over, the one named last changes fastest.
Arguments:
- voltages: bfloat16 [32, 2, 4096, 256], P('chan', None, ('row', 'col')), parts along dimension 0
- model: bfloat16 [32, 2, 4096, 4096], P('chan', None, 'row', 'col'), parts along dimension 0, as said below
Outputs:
- gains: float32 [32, 2, 4096], P('chan', None, 'col'), parts along dimension 0
- misfit: float32 [32, 4096], P('chan', 'col'), parts along dimension 0
There are 4 independent parts, one for each index of `chan`. A program takes and returns all parts, laid end to end along the dimension named above; each array names one. Nothing has to cross between parts.
Inputs may be any that keep to these rules, and one draw needn't show every extreme that they name: In every channel the model matrix is Hermitian: its real part is symmetric and its imaginary part antisymmetric.
All inputs are finite; a program needn't handle non-finite values.
Results may differ from a plain program's by a relative error of at most 0.0003.
Values may be sent and summed in bfloat16 or wider, within the bound.
A program may use at most 192 MiB of HBM per device.

v0:
```python
import jax
import jax.numpy as jnp
from jax import lax
from jax.sharding import PartitionSpec as P

ITERS = 3


EPSILON = 1e-06


def spread(block, axis, owner):
    block = jnp.where(lax.axis_index(axis) == owner, block, jnp.zeros_like(block))
    return lax.psum(block, axis)


def per_device(voltages, model):
    row_count = lax.axis_size("row")
    col_count = lax.axis_size("col")
    row_per_col = row_count // col_count
    row_index = lax.axis_index("row")
    col_index = lax.axis_index("col")
    channels = voltages.shape[0]
    shard_rows = voltages.shape[2]
    samples = voltages.shape[3]
    row_width = shard_rows * col_count
    col_width = row_width * row_per_col
    row_volts = lax.all_gather(voltages, "col", axis=2, tiled=True)
    members = []
    for member in range(row_per_col):
        members.append(spread(row_volts, "row", row_per_col * col_index + member))
    col_volts = jnp.concatenate(members, axis=2)
    left_side = jnp.concatenate(
        [
            jnp.concatenate([row_volts[:, 0], row_volts[:, 1]], axis=2),
            jnp.concatenate([row_volts[:, 1], -row_volts[:, 0]], axis=2),
        ],
        axis=1,
    )
    right_side = jnp.concatenate([col_volts[:, 0], col_volts[:, 1]], axis=2)
    product = lax.dot_general(
        left_side, right_side, (((2,), (2,)), ((0,), (0,))), preferred_element_type=jnp.float32
    ) * (1.0 / samples)
    vis_real = product[:, :row_width]
    vis_imag = product[:, row_width:]
    mod_real = model[:, 0].astype(jnp.float32)
    mod_imag = model[:, 1].astype(jnp.float32)
    global_rows = row_index * row_width + jnp.arange(row_width, dtype=jnp.int32)
    global_cols = col_index * col_width + jnp.arange(col_width, dtype=jnp.int32)
    off_diag = (global_rows[:, None] != global_cols[None, :]).astype(jnp.float32)
    row_re = jnp.ones((channels, row_width), jnp.float32)
    row_im = jnp.zeros((channels, row_width), jnp.float32)
    col_re = jnp.ones((channels, col_width), jnp.float32)
    col_im = jnp.zeros((channels, col_width), jnp.float32)
    for iteration in range(ITERS):
        along_re = row_re[:, :, None] * mod_real - row_im[:, :, None] * mod_imag
        along_im = row_re[:, :, None] * mod_imag + row_im[:, :, None] * mod_real
        local_re = jnp.sum(off_diag * (vis_real * along_re + vis_imag * along_im), axis=1)
        local_im = jnp.sum(off_diag * (vis_real * along_im - vis_imag * along_re), axis=1)
        local_den = jnp.sum(off_diag * (along_re * along_re + along_im * along_im), axis=1)
        numer_re, numer_im, denom = lax.psum((local_re, local_im, local_den), "row")
        fresh_re = numer_re / (denom + EPSILON)
        fresh_im = numer_im / (denom + EPSILON)
        if iteration % 2 == 1:
            fresh_re = (fresh_re + col_re) * 0.5
            fresh_im = (fresh_im + col_im) * 0.5
        col_re = fresh_re
        col_im = fresh_im
        offset = row_index % row_per_col * row_width
        slice_re = lax.dynamic_slice_in_dim(col_re, offset, row_width, 1)
        slice_im = lax.dynamic_slice_in_dim(col_im, offset, row_width, 1)
        row_re, row_im = (
            spread(slice_re, "col", row_index // row_per_col),
            spread(slice_im, "col", row_index // row_per_col),
        )
    along_re = row_re[:, :, None] * mod_real - row_im[:, :, None] * mod_imag
    along_im = row_re[:, :, None] * mod_imag + row_im[:, :, None] * mod_real
    error_re = vis_real - (along_re * col_re[:, None, :] + along_im * col_im[:, None, :])
    error_im = vis_imag - (along_im * col_re[:, None, :] - along_re * col_im[:, None, :])
    local_misfit = jnp.sum(off_diag * (error_re * error_re + error_im * error_im), axis=1)
    misfit = lax.psum(local_misfit, "row") / (row_width * row_count - 1)
    return (jnp.stack([col_re, col_im], axis=1), misfit)


def solution(mesh):
    return jax.shard_map(
        per_device,
        mesh=mesh,
        in_specs=(P("chan", None, ("row", "col"), None), P("chan", None, "row", "col")),
        out_specs=(P("chan", None, "col"), P("chan", "col")),
        check_vma=False,
    )
```

profile of v0, /device:TPU:8, one launch (start us, length us, event | category | flops | bytes accessed | tf_op | source)
XLA Modules:
  0.0 971.3 jit_solution(12483881551656533638)
XLA Ops:
  7.2 0.0 all-gather.2.cloned.1.call-start
  7.2 1.7 copy.8
  8.9 0.0 all-gather.2.cloned.1.call-update
  8.9 0.0 all-reduce.9.cloned.1.call-start
  9.0 49.7 %all-gather.2.cloned.1.call-done = bf16[8,2,256,256]{3,2,0,1:T(8,128)(2,1)} async-done(((bf16[8,2,32,256]{3,2,0,1:T(8,128)(2,1)}), bf16[8,2,256,256]{3,2,0,1:T(8,128)(2,1)}) %all-gather.2.cloned.1.call-update) | async-done | bytes 2097168 | tf_op jit(solution)/shard_map/all_gather | solution.py:28
  58.6 3.9 broadcast_select_fusion
  62.5 0.0 all-reduce.9.cloned.1.call-update
  62.6 0.1 compare_convert_fusion
  62.7 2.3 fusion.28
  65.0 3.1 slice_bitcast_fusion.3
  68.1 407.6 %all-reduce.9.cloned.1.call-done = (bf16[8,2,256,256]{3,2,0,1:T(8,128)(2,1)}, bf16[8,2,256,256]{3,2,0,1:T(8,128)(2,1)}) async-done(((bf16[8,2,256,256]{3,2,0,1:T(8,128)(2,1)}, bf16[8,2,256,256]{3,2,0,1:T(8,128)(2,1)}), (bf16[8,2,256,256]{3,2,0,1:T(8,128)(2,1)}, bf16[8,2,256,256]{3,2,0,1:T(8,128)(2,1)})) %all-reduce.9.cloned.1.call-update) | async-done | bytes 4194320 | tf_op jit(solution)/shard_map/psum | solution.py:14
  475.7 0.0 copy-start.1
  475.7 1.9 constant_dynamic-update-slice_fusion.1
  477.7 0.3 copy-done.1
  478.0 0.1 constant_dynamic-update-slice_fusion
  478.1 2.3 slice_bitcast_fusion.1
  480.4 4.8 broadcast_multiply_fusion
  485.2 0.0 copy-start
  485.2 6.8 multiply_reduce_fusion.9
  492.0 0.0 copy-done
  492.0 96.1 %all-reduce.2 = (f32[8,512]{1,0:T(8,128)S(1)}, f32[8,512]{1,0:T(8,128)S(1)}, f32[8,512]{1,0:T(8,128)S(1)}) all-reduce(f32[8,512]{1,0:T(8,128)S(1)} %get-tuple-element.9, f32[8,512]{1,0:T(8,128)S(1)} %get-tuple-element.12, f32[8,512]{1,0:T(8,128)S(1)} %get-tuple-element.8), channel_id=1, replica_groups=mesh['chan'=4,'row'=16,'col'=8] {'row'}, use_global_device_ids=true, to_apply=%region_8.9 | all-reduce | flops 12288 | bytes 98304 | tf_op jit(solution)/shard_map/psum | solution.py:61
  588.2 25.9 %all-reduce.5 = (f32[8,256]{1,0:T(8,128)S(1)}, f32[8,256]{1,0:T(8,128)S(1)}) all-reduce(f32[8,256]{1,0:T(8,128)S(1)} %get-tuple-element.42, f32[8,256]{1,0:T(8,128)S(1)} %get-tuple-element.43), channel_id=1, replica_groups=mesh['chan'=4,'row'=16,'col'=8] {'col'}, use_global_device_ids=true, to_apply=%region_9.10 | all-reduce | flops 4096 | bytes 32768 | tf_op jit(solution)/shard_map/psum | solution.py:14
  614.1 6.8 multiply_reduce_fusion.6
  620.9 91.3 %all-reduce.1 = (f32[8,512]{1,0:T(8,128)S(1)}, f32[8,512]{1,0:T(8,128)S(1)}, f32[8,512]{1,0:T(8,128)S(1)}) all-reduce(f32[8,512]{1,0:T(8,128)S(1)} %get-tuple-element.7, f32[8,512]{1,0:T(8,128)S(1)} %get-tuple-element.11, f32[8,512]{1,0:T(8,128)S(1)} %get-tuple-element.6), channel_id=1, replica_groups=mesh['chan'=4,'row'=16,'col'=8] {'row'}, use_global_device_ids=true, to_apply=%region_16.17 | all-reduce | flops 12288 | bytes 98304 | tf_op jit(solution)/shard_map/psum | solution.py:61
  712.3 25.9 %all-reduce.4 = (f32[8,256]{1,0:T(8,128)S(1)}, f32[8,256]{1,0:T(8,128)S(1)}) all-reduce(f32[8,256]{1,0:T(8,128)S(1)} %get-tuple-element.39, f32[8,256]{1,0:T(8,128)S(1)} %get-tuple-element.38), channel_id=1, replica_groups=mesh['chan'=4,'row'=16,'col'=8] {'col'}, use_global_device_ids=true, to_apply=%region_17.18 | all-reduce | flops 4096 | bytes 32768 | tf_op jit(solution)/shard_map/psum | solution.py:14
  738.2 6.8 multiply_reduce_fusion.3
  745.0 94.7 %all-reduce = (f32[8,512]{1,0:T(8,128)S(1)}, f32[8,512]{1,0:T(8,128)S(1)}, f32[8,512]{1,0:T(8,128)S(1)}) all-reduce(f32[8,512]{1,0:T(8,128)S(1)} %get-tuple-element.5, f32[8,512]{1,0:T(8,128)S(1)} %get-tuple-element.10, f32[8,512]{1,0:T(8,128)S(1)} %get-tuple-element.4), channel_id=1, replica_groups=mesh['chan'=4,'row'=16,'col'=8] {'row'}, use_global_device_ids=true, to_apply=%region_23.24 | all-reduce | flops 12288 | bytes 98304 | tf_op jit(solution)/shard_map/psum | solution.py:61
  839.8 25.9 %all-reduce.3 = (f32[8,256]{1,0:T(8,128)S(1)}, f32[8,256]{1,0:T(8,128)S(1)}) all-reduce(f32[8,256]{1,0:T(8,128)S(1)} %dynamic-slice_select_fusion, f32[8,256]{1,0:T(8,128)S(1)} %dynamic-slice_select_fusion.1), channel_id=1, replica_groups=mesh['chan'=4,'row'=16,'col'=8] {'col'}, use_global_device_ids=true, to_apply=%region_25.26 | all-reduce | flops 4096 | bytes 32768 | tf_op jit(solution)/shard_map/psum | solution.py:14
  865.7 6.2 multiply_reduce_fusion
  871.9 91.3 %psum.143 = f32[8,512]{1,0:T(8,128)S(1)} all-reduce(f32[8,512]{1,0:T(8,128)S(1)} %multiply_reduce_fusion), channel_id=1, replica_groups=mesh['chan'=4,'row'=16,'col'=8] {'row'}, use_global_device_ids=true, to_apply=%region_27.28 | all-reduce | flops 4096 | bytes 32768 | tf_op jit(solution)/shard_map/psum | solution.py:81
  963.2 0.6 broadcast_multiply_fusion.1
  963.8 0.6 copy.11
  (10 shorter events, 0.1 us)
Async XLA Ops:
  7.2 51.5 %all-gather.2.cloned.1.call-start = ((), (), s32[]{:S(2)}) async-start(), calls=%async_computation | async-start | bytes 2359296 | tf_op jit(solution)/shard_map/all_gather | solution.py:28
  8.9 466.8 %all-reduce.9.cloned.1.call-start = ((), (), s32[]{:S(2)}) async-start(), calls=%async_computation.1 | async-start | bytes 8388608 | tf_op jit(solution)/shard_map/psum | solution.py:14
  475.7 2.2 copy-start.1
  485.2 6.8 copy-start
Sparse Core Ops, SparseCore 0:
  10.1 48.5 all-gather.1
  62.7 413.0 all-reduce.8
where the time goes:
time: 972 us; the launch traced here: 971 us
  waiting for transfers between devices  457 us (47%)
  blocking collectives  451 us (46%)
  other arithmetic  33.5 us (3%)
  between operations  14.2 us (1%)
  local copies, waits for them, and re-layouts  10.1 us (1%)
    psum x1, waiting for transfers between devices, spread(): return lax.psum(block, axis)  408 us
    psum x3, blocking collectives, per_device(): numer_re, numer_im, denom = lax.psum((local_re, local_im, local_den), 'row')  282 us
    psum x1, blocking collectives, per_device(): misfit = lax.psum(local_misfit, 'row') / (row_width * row_count - 1)  91.3 us
    psum x3, blocking collectives, spread(): return lax.psum(block, axis)  77.8 us
    all_gather x1, waiting for transfers between devices, per_device(): row_volts = lax.all_gather(voltages, 'col', axis=2, tiled=True)  49.7 us
    reduce_sum x3, other arithmetic, per_device(): jnp.sum(off_diag * (vis_real * along_re + vis_imag * along_im), axis=1)  20.4 us
  transfers between devices with their start and end apart: 2, of which 2 were waited for; matrix products, arithmetic and copies ran while one was open for 1% of the time, Pallas kernels for 0%

commit v1 on v0

v1 whole, which is shorter than its diff:
```python
import functools

import jax
import jax.numpy as jnp
from jax import lax
from jax.experimental import pallas as pl
from jax.experimental.pallas import tpu as pltpu
from jax.sharding import PartitionSpec as P

EPSILON = 1e-06
MESH = pl.DeviceIdType.MESH
F32 = jnp.float32

RING = 16
SEG = 4
XS = 4
LINE = 2 * RING
HALF = RING
CHUNKS = 2
STEPS = (RING // 2 + 1) * CHUNKS
ROWS = 16
TILE = (8, 128)


def div(a, b):
    return lax.div(a, jnp.int32(b))


def rem(a, b):
    return lax.rem(a, jnp.int32(b))


def kernel(
    volts, model, gains_out, misfit_out,
    buf, mod, vis, spread, sbuf, rbuf, total, gtile, gbuf, cbuf, mtile, mbuf,
    load_sem, ring_send, ring_recv, sib_send, sib_recv, chain_send, chain_recv,
    part_send, part_recv, gain_send, gain_recv, col_send, col_recv, mis_send, mis_recv,
):
    channels = mod.shape[0]
    samples = volts.shape[3]
    per_chunk = channels // CHUNKS
    inputs = 4096
    r = lax.axis_index("row")
    c = lax.axis_index("col")
    x, zh = div(r, SEG), rem(r, SEG)
    zl, k = div(c, 2), rem(c, 2)
    z = zh * SEG + zl
    hub = x == zl
    odd = rem(r, 2)
    own_row = div(r, 2) == c

    def place(xx, zz, kk):
        return {"row": xx * SEG + div(zz, SEG), "col": rem(zz, SEG) * 2 + kk}

    own_slot = z * 2 + k
    load_volts = pltpu.make_async_copy(volts, buf.at[own_slot], load_sem.at[0])
    load_model = pltpu.make_async_copy(model, mod, load_sem.at[1])
    load_volts.start()
    load_model.start()

    barrier = pltpu.get_barrier_semaphore()

    def signal(target):
        pl.semaphore_signal(barrier, inc=1, device_id=target, device_id_type=MESH)

    signal(place(x, rem(z + 1, RING), k))
    signal(place(x, rem(z + RING - 1, RING), k))
    signal(place(x, z, 1 - k))

    def greet(i, _):
        @pl.when(i != r)
        def _():
            signal({"row": i, "col": c})
        return 0

    lax.fori_loop(0, 2 * channels, greet, 0)

    def greet_owner(ch, _):
        @pl.when(jnp.logical_not(jnp.logical_and(own_row, ch == c)))
        def _():
            signal({"row": 2 * ch + odd, "col": div(r, 2)})
        return 0

    lax.fori_loop(0, channels, greet_owner, 0)
    sbuf[...] = jnp.zeros(sbuf.shape, F32)
    gtile[...] = jnp.zeros(gtile.shape, F32)
    mtile[...] = jnp.zeros(mtile.shape, F32)
    load_volts.wait()
    pl.semaphore_wait(barrier, 3 + 2 * channels - 1 + channels - own_row.astype(jnp.int32))

    def chunk(slot, q):
        return buf.at[slot, pl.ds(q * per_chunk, per_chunk)]

    def reach(way, q):
        return RING // 2 - rem(q + way, 2)

    def shard(way, t):
        return rem(z - t + RING, RING) if way == 0 else rem(z + t, RING)

    def exists(way, t, q):
        here = t <= reach(way, q)
        return here if way == 0 else jnp.logical_and(here, t >= 1)

    def ring_copy(way, n):
        t, q = div(n, CHUNKS), rem(n, CHUNKS)
        slot = shard(way, t) * 2 + k
        nxt = rem(z + 1, RING) if way == 0 else rem(z + RING - 1, RING)
        return pltpu.make_async_remote_copy(
            src_ref=chunk(slot, q), dst_ref=chunk(slot, q),
            send_sem=ring_send.at[way, n], recv_sem=ring_recv.at[way, n + CHUNKS],
            device_id=place(x, nxt, k), device_id_type=MESH)

    def arrival(slot, q, sem):
        return pltpu.make_async_copy(chunk(slot, q), chunk(slot, q), sem)

    def sib_copy(way, n):
        t, q = div(n, CHUNKS), rem(n, CHUNKS)
        slot = shard(way, t) * 2 + k
        return pltpu.make_async_remote_copy(
            src_ref=chunk(slot, q), dst_ref=chunk(slot, q),
            send_sem=sib_send.at[way, n], recv_sem=sib_recv.at[way, n],
            device_id=place(x, z, 1 - k), device_id_type=MESH)

    def sib_wanted(way, n, core):
        t, q = div(n, CHUNKS), rem(n, CHUNKS)
        zz = shard(way, t)
        use = jnp.logical_or(
            div(zz, SEG) == zh, jnp.logical_and(hub, div(zz, RING // 2) == core))
        return jnp.logical_and(exists(way, t, q), use)

    def chain_place(core):
        if core == 0:
            return rem(x - zl + XS, XS), rem(x + 1, XS)
        return rem(zl - x + XS, XS), rem(x + XS - 1, XS)

    def chain_copy(core, way, m):
        t, q = div(m, CHUNKS), rem(m, CHUNKS)
        zz = shard(way, t)
        _, nxt = chain_place(core)
        to = LINE + rem(zz, RING // 2) * 2 + core
        slot = jnp.where(hub, zz * 2 + core, to)
        return pltpu.make_async_remote_copy(
            src_ref=chunk(slot, q), dst_ref=chunk(to, q),
            send_sem=chain_send.at[core, way, m], recv_sem=chain_recv.at[core, way, m],
            device_id=place(nxt, z, k), device_id_type=MESH)

    def chain_wanted(way, m):
        t, q = div(m, CHUNKS), rem(m, CHUNKS)
        mine = div(shard(way, t), RING // 2) == k
        inside = jnp.logical_and(m >= 0, m < STEPS)
        return jnp.logical_and(inside, jnp.logical_and(exists(way, t, q), mine))

    def gather(n, _):
        t, q = div(n, CHUNKS), rem(n, CHUNKS)
        for way in (0, 1):
            @pl.when(jnp.logical_and(n < STEPS, t <= reach(way, q)))
            def _():
                @pl.when(t >= 1)
                def _():
                    arrival(shard(way, t) * 2 + k, q, ring_recv.at[way, n]).wait()

                @pl.when(t < reach(way, q))
                def _():
                    ring_copy(way, n).start()

                @pl.when(sib_wanted(way, n, 1 - k))
                def _():
                    sib_copy(way, n).start()
        m = jnp.maximum(n - 1, 0)
        for way in (0, 1):
            @pl.when(jnp.logical_and(jnp.logical_and(n >= 1, n <= STEPS), sib_wanted(way, m, k)))
            def _():
                arrival(shard(way, div(m, CHUNKS)) * 2 + 1 - k, rem(m, CHUNKS), sib_recv.at[way, m]).wait()
        for core in (0, 1):
            far, _ = chain_place(core)
            raw = n - 1 - far
            m = jnp.maximum(raw, 0)
            for way in (0, 1):
                @pl.when(jnp.logical_and(raw >= 0, chain_wanted(way, m)))
                def _():
                    @pl.when(far >= 1)
                    def _():
                        zz = shard(way, div(m, CHUNKS))
                        slot = LINE + rem(zz, RING // 2) * 2 + core
                        arrival(slot, rem(m, CHUNKS), chain_recv.at[core, way, m]).wait()

                    @pl.when(far < XS - 1)
                    def _():
                        chain_copy(core, way, m).start()
        return 0

    lax.fori_loop(0, STEPS + XS, gather, 0)

    def settle(n, _):
        t, q = div(n, CHUNKS), rem(n, CHUNKS)
        for way in (0, 1):
            @pl.when(t < reach(way, q))
            def _():
                ring_copy(way, n).wait_send()

            @pl.when(sib_wanted(way, n, 1 - k))
            def _():
                sib_copy(way, n).wait_send()

            for core in (0, 1):
                far, _ = chain_place(core)

                @pl.when(jnp.logical_and(far < XS - 1, chain_wanted(way, n)))
                def _():
                    chain_copy(core, way, n).wait_send()
        return 0

    width = vis.shape[3]
    height = vis.shape[2]
    half = width // 2
    lanes = TILE[1]
    row_base = zh * (2 * SEG)
    col_base = jnp.where(hub, k * HALF, LINE)
    load_model.wait()

    def part_copy(phase, target):
        return pltpu.make_async_remote_copy(
            src_ref=sbuf.at[phase, target], dst_ref=rbuf.at[phase, r],
            send_sem=part_send.at[phase], recv_sem=part_recv.at[phase],
            device_id={"row": target, "col": c}, device_id_type=MESH)

    def hand_in(phase, target):
        @pl.when(target != r)
        def _():
            part_copy(phase, target).start()

        @pl.when(target == r)
        def _():
            rbuf[phase, r] = sbuf[phase, r]

    def put(phase, target, first, value):
        for j in range(half // lanes):
            sbuf[phase, target, first + j : first + j + 1, :] = value[:, j * lanes : (j + 1) * lanes]

    def fold(value):
        return jnp.sum(value.reshape(ROWS // 8, 8, half), axis=0)

    def wide(value):
        return jnp.concatenate([value] * (half // lanes), axis=1)

    def along(ch, rows, cols, plain):
        mr = mod[ch, 0, rows, cols].astype(F32)
        mi = mod[ch, 1, rows, cols].astype(F32)
        if plain:
            return mr, mi
        gr = wide(spread[ch, 0, rows, :])
        gi = wide(spread[ch, 1, rows, :])
        return gr * mr - gi * mi, gr * mi + gi * mr

    def normal_sums(phase, ch):
        for b in (0, 1):
            cols = slice(b * half, (b + 1) * half)

            def body(i, acc):
                rows = pl.ds(pl.multiple_of(i * ROWS, ROWS), ROWS)
                vr = vis[ch, 0, rows, cols]
                vi = vis[ch, 1, rows, cols]
                ar, ai = along(ch, rows, cols, phase == 0)
                return (
                    acc[0] + fold(vr * ar + vi * ai),
                    acc[1] + fold(vr * ai - vi * ar),
                    acc[2] + fold(ar * ar + ai * ai),
                )

            zero = jnp.zeros((8, half), F32)
            sums = lax.fori_loop(0, height // ROWS, body, (zero, zero, zero), unroll=4)
            for i, value in enumerate(sums):
                put(phase, 2 * ch + b, 2 * i, jnp.sum(value, axis=0, keepdims=True))
            hand_in(phase, 2 * ch + b)

    def misfit_sums(phase, ch):
        for b in (0, 1):
            cols = slice(b * half, (b + 1) * half)
            cr = jnp.concatenate([cbuf[2 * ch + b, 0:1, :], cbuf[2 * ch + b, 1:2, :]], axis=1)
            ci = jnp.concatenate([cbuf[2 * ch + b, 2:3, :], cbuf[2 * ch + b, 3:4, :]], axis=1)

            def body(i, acc):
                rows = pl.ds(pl.multiple_of(i * ROWS, ROWS), ROWS)
                ar, ai = along(ch, rows, cols, False)
                er = vis[ch, 0, rows, cols] - (ar * cr + ai * ci)
                ei = vis[ch, 1, rows, cols] - (ai * cr - ar * ci)
                return acc + fold(er * er + ei * ei)

            total_here = lax.fori_loop(0, height // ROWS, body, jnp.zeros((8, half), F32), unroll=4)
            put(phase, 2 * ch + b, 0, jnp.sum(total_here, axis=0, keepdims=True))
            hand_in(phase, 2 * ch + b)

    def no_diagonal(ref, ch):
        for b in (0, 1):
            @pl.when(jnp.logical_and(own_row, odd == b))
            def _():
                for comp in (0, 1):
                    def body(i, _):
                        for j in range(half // lanes):
                            rows = pl.ds(pl.multiple_of(j * lanes + i * ROWS, ROWS), ROWS)
                            cols = slice(b * half + j * lanes, b * half + (j + 1) * lanes)
                            row_id = lax.broadcasted_iota(jnp.int32, (ROWS, lanes), 0) + i * ROWS
                            col_id = lax.broadcasted_iota(jnp.int32, (ROWS, lanes), 1)
                            tile = ref[ch, comp, rows, cols].astype(F32)
                            ref[ch, comp, rows, cols] = jnp.where(row_id == col_id, 0.0, tile).astype(ref.dtype)
                        return 0

                    lax.fori_loop(0, lanes // ROWS, body, 0)

    def first(ch, _):
        row_re = buf[pl.ds(row_base, 2 * SEG), ch, 0].reshape(height, samples)
        row_im = buf[pl.ds(row_base, 2 * SEG), ch, 1].reshape(height, samples)
        col_re = buf[pl.ds(col_base, HALF), ch, 0].reshape(width, samples)
        col_im = buf[pl.ds(col_base, HALF), ch, 1].reshape(width, samples)

        def gram(a, b):
            return lax.dot_general(a, b, (((1,), (1,)), ((), ())), preferred_element_type=F32)

        vis[ch, 0] = (gram(row_re, col_re) + gram(row_im, col_im)) * (1.0 / samples)
        vis[ch, 1] = (gram(row_im, col_re) - gram(row_re, col_im)) * (1.0 / samples)
        no_diagonal(vis, ch)
        no_diagonal(mod, ch)
        normal_sums(0, ch)
        return 0

    def collect(phase):
        part = rbuf.at[phase, pl.ds(0, 2 * channels - 1)]
        pltpu.make_async_copy(part, part, part_recv.at[phase]).wait()
        total[...] = jnp.sum(rbuf[phase], axis=0)

    def gain_copy(phase, i):
        return pltpu.make_async_remote_copy(
            src_ref=gtile.at[phase], dst_ref=gbuf.at[phase, div(r, 2)],
            send_sem=gain_send.at[phase], recv_sem=gain_recv.at[phase, div(r, 2)],
            device_id={"row": 2 * c + odd, "col": i}, device_id_type=MESH)

    def col_copy(tile, dst, send, recv, i):
        return pltpu.make_async_remote_copy(
            src_ref=tile, dst_ref=dst.at[r], send_sem=send, recv_sem=recv,
            device_id={"row": i, "col": c}, device_id_type=MESH)

    def to_column(tile, dst, send, recv):
        def body(i, _):
            @pl.when(i != r)
            def _():
                col_copy(tile, dst, send, recv, i).start()
            return 0

        lax.fori_loop(0, 2 * channels, body, 0)
        dst[r] = tile[...]

    def wait_column(dst, sem):
        part = dst.at[pl.ds(0, 2 * channels - 1)]
        pltpu.make_async_copy(part, part, sem).wait()

    def own_gains(phase):
        collect(phase)
        den = total[4:6, :] + EPSILON
        fresh_re = total[0:2, :] / den
        fresh_im = total[2:4, :] / den
        if phase % 2 == 1:
            fresh_re = (fresh_re + gtile[phase - 1, 0:2, :]) * 0.5
            fresh_im = (fresh_im + gtile[phase - 1, 2:4, :]) * 0.5
        gtile[phase, 0:2, :] = fresh_re
        gtile[phase, 2:4, :] = fresh_im

        def body(i, _):
            @pl.when(jnp.logical_not(jnp.logical_and(own_row, i == c)))
            def _():
                gain_copy(phase, i).start()
            return 0

        lax.fori_loop(0, channels, body, 0)

        @pl.when(own_row)
        def _():
            gbuf[phase, div(r, 2)] = gtile[phase]

    def take_gains(phase, ch):
        @pl.when(jnp.logical_not(jnp.logical_and(own_row, ch == c)))
        def _():
            part = gbuf.at[phase, ch]
            pltpu.make_async_copy(part, part, gain_recv.at[phase, ch]).wait()
        for comp in (0, 1):
            for j in range(height // lanes):
                line = gbuf[phase, ch, 2 * comp + j : 2 * comp + j + 1, :]
                spread[ch, comp, j * lanes : (j + 1) * lanes, :] = jnp.broadcast_to(line, (lanes, lanes)).T

    lax.fori_loop(0, channels, first, 0)
    own_gains(0)
    for phase in (1, 2):
        def again(ch, _):
            take_gains(phase - 1, ch)
            normal_sums(phase, ch)
            return 0

        lax.fori_loop(0, channels, again, 0)
        own_gains(phase)
    to_column(gtile.at[2], cbuf, col_send, col_recv)

    def last(ch, _):
        take_gains(2, ch)
        misfit_sums(3, ch)
        return 0

    wait_column(cbuf, col_recv)
    lax.fori_loop(0, channels, last, 0)
    collect(3)
    mtile[0:2, :] = total[0:2, :] / (inputs - 1)
    to_column(mtile, mbuf, mis_send, mis_recv)
    for ch in range(channels):
        for b in (0, 1):
            for j in range(half // lanes):
                cols = slice(b * half + j * lanes, b * half + (j + 1) * lanes)
                for comp in (0, 1):
                    gains_out[ch, comp : comp + 1, cols] = cbuf[2 * ch + b, 2 * comp + j : 2 * comp + j + 1, :]

    lax.fori_loop(0, STEPS, settle, 0)
    for phase in range(4):
        part = sbuf.at[phase, pl.ds(0, 2 * channels - 1)]
        pltpu.make_async_copy(part, part, part_send.at[phase]).wait()
    for phase in range(3):
        for sent, there in ((channels - 1, own_row), (channels, jnp.logical_not(own_row))):
            @pl.when(there)
            def _():
                part = gbuf.at[phase, pl.ds(0, sent)]
                pltpu.make_async_copy(part, part, gain_send.at[phase]).wait()
    wait_column(cbuf, col_send)
    wait_column(mbuf, mis_send)
    wait_column(mbuf, mis_recv)
    for ch in range(channels):
        for b in (0, 1):
            for j in range(half // lanes):
                cols = slice(b * half + j * lanes, b * half + (j + 1) * lanes)
                misfit_out[ch : ch + 1, cols] = mbuf[2 * ch + b, j : j + 1, :]


def per_device(voltages, model):
    channels, _, shard_rows, samples = voltages.shape
    height, width = model.shape[2:]
    dma = pltpu.SemaphoreType.DMA
    return pl.pallas_call(
        kernel,
        out_shape=(
            jax.ShapeDtypeStruct((channels, 2, width), F32),
            jax.ShapeDtypeStruct((channels, width), F32),
        ),
        in_specs=[pl.BlockSpec(memory_space=pl.ANY)] * 2,
        out_specs=(pl.BlockSpec(memory_space=pltpu.VMEM),) * 2,
        scratch_shapes=[
            pltpu.VMEM((LINE + HALF,) + voltages.shape, voltages.dtype),
            pltpu.VMEM(model.shape, model.dtype),
            pltpu.VMEM((channels, 2, height, width), F32),
            pltpu.VMEM((channels, 2, height, TILE[1]), F32),
            pltpu.VMEM((4, 2 * channels) + TILE, F32),
            pltpu.VMEM((4, 2 * channels) + TILE, F32),
            pltpu.VMEM(TILE, F32),
            pltpu.VMEM((3,) + TILE, F32),
            pltpu.VMEM((3, channels) + TILE, F32),
            pltpu.VMEM((2 * channels,) + TILE, F32),
            pltpu.VMEM(TILE, F32),
            pltpu.VMEM((2 * channels,) + TILE, F32),
            dma((2,)),
            dma((2, STEPS)),
            dma((2, STEPS)),
            dma((2, STEPS)),
            dma((2, STEPS)),
            dma((2, 2, STEPS)),
            dma((2, 2, STEPS)),
            dma((4,)),
            dma((4,)),
            dma((3,)),
            dma((3, channels)),
            dma(()),
            dma(()),
            dma(()),
            dma(()),
        ],
        compiler_params=pltpu.CompilerParams(
            collective_id=0, has_side_effects=True, vmem_limit_bytes=50 * 2**20
        ),
    )(voltages, model)


def solution(mesh):
    return jax.shard_map(
        per_device,
        mesh=mesh,
        in_specs=(P("chan", None, ("row", "col"), None), P("chan", None, "row", "col")),
        out_specs=(P("chan", None, "col"), P("chan", "col")),
        check_vma=False,
    )
```

time: 972 us -> 176 us (0.18)
  the two profiles are of different devices: /device:TPU:8 before, /device:TPU:48 now
where the time goes in v1:
time: 176 us; the launch traced here: 175 us
  Pallas kernels  173 us (98%)
  local copies, waits for them, and re-layouts  2.17 us (1%)
    pallas_call x1, Pallas kernels, per_device(): pl.pallas_call(kernel, out_shape=(jax.ShapeDtypeStruct((channels, 2, widt...  173 us

profile of v1, /device:TPU:48, one launch (start us, length us, event | category | flops | bytes accessed | tf_op | source)
XLA Modules:
  0.0 175.5 jit_solution(2667067370719879310)
XLA Ops:
  0.6 0.0 copy-start
  0.6 0.9 copy-done
  1.6 172.6 %shard_map.41 = (f32[8,2,512]{2,1,0:T(2,128)S(1)}, f32[8,512]{1,0:T(8,128)S(1)}) custom-call(bf16[8,2,32,256]{3,2,1,0:T(8,128)(2,1)S(1)} %copy-done, bf16[8,2,256,512]{3,2,1,0:T(8,128)(2,1)} %model.1), custom_call_target="tpu_custom_call" | custom-call | tf_op jit(solution)/shard_map/pallas_call | solution.py:442
  174.2 0.6 copy.6
  174.8 0.6 copy.7
Async XLA Ops:
  0.6 1.0 copy-start

commit v2 on v1

--- a/solution.py
+++ b/solution.py
@@ -16,9 +16,12 @@
 XS = 4
 LINE = 2 * RING
 HALF = RING
-CHUNKS = 2
-STEPS = (RING // 2 + 1) * CHUNKS
-ROWS = 16
+GROUPS = 2
+SUBS = 2
+SPAN = (RING // 2 + 1) * SUBS
+STEPS = GROUPS * SPAN
+LAG = 2
+ROWS = 32
 TILE = (8, 128)
 
 
@@ -38,7 +41,8 @@
 ):
     channels = mod.shape[0]
     samples = volts.shape[3]
-    per_chunk = channels // CHUNKS
+    per_chunk = channels // (GROUPS * SUBS)
+    per_group = channels // GROUPS
     inputs = 4096
     r = lax.axis_index("row")
     c = lax.axis_index("col")
@@ -47,6 +51,7 @@
     z = zh * SEG + zl
     hub = x == zl
     odd = rem(r, 2)
+    own_group = div(r, 2 * per_group)
     own_row = div(r, 2) == c
 
     def place(xx, zz, kk):
@@ -88,33 +93,37 @@
     load_volts.wait()
     pl.semaphore_wait(barrier, 3 + 2 * channels - 1 + channels - own_row.astype(jnp.int32))
 
+    def split(n):
+        sub = rem(n, SUBS)
+        return div(rem(n, SPAN), SUBS), sub, div(n, SPAN) * SUBS + sub
+
     def chunk(slot, q):
         return buf.at[slot, pl.ds(q * per_chunk, per_chunk)]
 
-    def reach(way, q):
-        return RING // 2 - rem(q + way, 2)
+    def reach(way, sub):
+        return RING // 2 - rem(sub + way, 2)
 
     def shard(way, t):
         return rem(z - t + RING, RING) if way == 0 else rem(z + t, RING)
 
-    def exists(way, t, q):
-        here = t <= reach(way, q)
+    def exists(way, t, sub):
+        here = t <= reach(way, sub)
         return here if way == 0 else jnp.logical_and(here, t >= 1)
 
     def ring_copy(way, n):
-        t, q = div(n, CHUNKS), rem(n, CHUNKS)
+        t, sub, q = split(n)
         slot = shard(way, t) * 2 + k
         nxt = rem(z + 1, RING) if way == 0 else rem(z + RING - 1, RING)
         return pltpu.make_async_remote_copy(
             src_ref=chunk(slot, q), dst_ref=chunk(slot, q),
-            send_sem=ring_send.at[way, n], recv_sem=ring_recv.at[way, n + CHUNKS],
+            send_sem=ring_send.at[way, n], recv_sem=ring_recv.at[way, n + SUBS],
             device_id=place(x, nxt, k), device_id_type=MESH)
 
     def arrival(slot, q, sem):
         return pltpu.make_async_copy(chunk(slot, q), chunk(slot, q), sem)
 
     def sib_copy(way, n):
-        t, q = div(n, CHUNKS), rem(n, CHUNKS)
+        t, sub, q = split(n)
         slot = shard(way, t) * 2 + k
         return pltpu.make_async_remote_copy(
             src_ref=chunk(slot, q), dst_ref=chunk(slot, q),
@@ -122,11 +131,11 @@
             device_id=place(x, z, 1 - k), device_id_type=MESH)
 
     def sib_wanted(way, n, core):
-        t, q = div(n, CHUNKS), rem(n, CHUNKS)
+        t, sub, q = split(n)
         zz = shard(way, t)
         use = jnp.logical_or(
             div(zz, SEG) == zh, jnp.logical_and(hub, div(zz, RING // 2) == core))
-        return jnp.logical_and(exists(way, t, q), use)
+        return jnp.logical_and(exists(way, t, sub), use)
 
     def chain_place(core):
         if core == 0:
@@ -134,7 +143,7 @@
         return rem(zl - x + XS, XS), rem(x + XS - 1, XS)
 
     def chain_copy(core, way, m):
-        t, q = div(m, CHUNKS), rem(m, CHUNKS)
+        t, sub, q = split(m)
         zz = shard(way, t)
         _, nxt = chain_place(core)
         to = LINE + rem(zz, RING // 2) * 2 + core
@@ -145,56 +154,55 @@
             device_id=place(nxt, z, k), device_id_type=MESH)
 
     def chain_wanted(way, m):
-        t, q = div(m, CHUNKS), rem(m, CHUNKS)
+        t, sub, q = split(m)
         mine = div(shard(way, t), RING // 2) == k
         inside = jnp.logical_and(m >= 0, m < STEPS)
-        return jnp.logical_and(inside, jnp.logical_and(exists(way, t, q), mine))
-
-    def gather(n, _):
-        t, q = div(n, CHUNKS), rem(n, CHUNKS)
+        return jnp.logical_and(inside, jnp.logical_and(exists(way, t, sub), mine))
+
+    def gather(n):
+        t, sub, q = split(n)
         for way in (0, 1):
-            @pl.when(jnp.logical_and(n < STEPS, t <= reach(way, q)))
+            @pl.when(jnp.logical_and(n < STEPS, t <= reach(way, sub)))
             def _():
                 @pl.when(t >= 1)
                 def _():
                     arrival(shard(way, t) * 2 + k, q, ring_recv.at[way, n]).wait()
 
-                @pl.when(t < reach(way, q))
+                @pl.when(t < reach(way, sub))
                 def _():
                     ring_copy(way, n).start()
 
                 @pl.when(sib_wanted(way, n, 1 - k))
                 def _():
                     sib_copy(way, n).start()
-        m = jnp.maximum(n - 1, 0)
+        m = jnp.maximum(n - LAG, 0)
         for way in (0, 1):
-            @pl.when(jnp.logical_and(jnp.logical_and(n >= 1, n <= STEPS), sib_wanted(way, m, k)))
-            def _():
-                arrival(shard(way, div(m, CHUNKS)) * 2 + 1 - k, rem(m, CHUNKS), sib_recv.at[way, m]).wait()
+            @pl.when(jnp.logical_and(jnp.logical_and(n >= LAG, n < STEPS + LAG), sib_wanted(way, m, k)))
+            def _():
+                t, _, q = split(m)
+                arrival(shard(way, t) * 2 + 1 - k, q, sib_recv.at[way, m]).wait()
         for core in (0, 1):
             far, _ = chain_place(core)
-            raw = n - 1 - far
+            raw = n - LAG - LAG * far
             m = jnp.maximum(raw, 0)
             for way in (0, 1):
                 @pl.when(jnp.logical_and(raw >= 0, chain_wanted(way, m)))
                 def _():
                     @pl.when(far >= 1)
                     def _():
-                        zz = shard(way, div(m, CHUNKS))
+                        t, _, q = split(m)
+                        zz = shard(way, t)
                         slot = LINE + rem(zz, RING // 2) * 2 + core
-                        arrival(slot, rem(m, CHUNKS), chain_recv.at[core, way, m]).wait()
+                        arrival(slot, q, chain_recv.at[core, way, m]).wait()
 
                     @pl.when(far < XS - 1)
                     def _():
                         chain_copy(core, way, m).start()
-        return 0
-
-    lax.fori_loop(0, STEPS + XS, gather, 0)
 
     def settle(n, _):
-        t, q = div(n, CHUNKS), rem(n, CHUNKS)
+        t, sub, q = split(n)
         for way in (0, 1):
-            @pl.when(t < reach(way, q))
+            @pl.when(t < reach(way, sub))
             def _():
                 ring_copy(way, n).wait_send()
 
@@ -216,7 +224,6 @@
     lanes = TILE[1]
     row_base = zh * (2 * SEG)
     col_base = jnp.where(hub, k * HALF, LINE)
-    load_model.wait()
 
     def part_copy(phase, target):
         return pltpu.make_async_remote_copy(
@@ -307,21 +314,18 @@
 
                     lax.fori_loop(0, lanes // ROWS, body, 0)
 
-    def first(ch, _):
+    def correlate(ch):
         row_re = buf[pl.ds(row_base, 2 * SEG), ch, 0].reshape(height, samples)
         row_im = buf[pl.ds(row_base, 2 * SEG), ch, 1].reshape(height, samples)
         col_re = buf[pl.ds(col_base, HALF), ch, 0].reshape(width, samples)
         col_im = buf[pl.ds(col_base, HALF), ch, 1].reshape(width, samples)
 
-        def gram(a, b):
-            return lax.dot_general(a, b, (((1,), (1,)), ((), ())), preferred_element_type=F32)
-
-        vis[ch, 0] = (gram(row_re, col_re) + gram(row_im, col_im)) * (1.0 / samples)
-        vis[ch, 1] = (gram(row_im, col_re) - gram(row_re, col_im)) * (1.0 / samples)
-        no_diagonal(vis, ch)
-        no_diagonal(mod, ch)
-        normal_sums(0, ch)
-        return 0
+        left = jnp.concatenate(
+            [jnp.concatenate([row_re, row_im], axis=1), jnp.concatenate([row_im, -row_re], axis=1)], axis=0)
+        right = jnp.concatenate([col_re, col_im], axis=1)
+        product = lax.dot_general(left, right, (((1,), (1,)), ((), ())), preferred_element_type=F32) * (1.0 / samples)
+        vis[ch, 0] = product[:height]
+        vis[ch, 1] = product[height:]
 
     def collect(phase):
         part = rbuf.at[phase, pl.ds(0, 2 * channels - 1)]
@@ -343,13 +347,21 @@
         def body(i, _):
             @pl.when(i != r)
             def _():
-                col_copy(tile, dst, send, recv, i).start()
+                col_copy(tile, dst, send, recv.at[own_group], i).start()
             return 0
 
         lax.fori_loop(0, 2 * channels, body, 0)
         dst[r] = tile[...]
 
-    def wait_column(dst, sem):
+    def wait_column(dst, recv, group):
+        tiles = 2 * per_group
+        for count, there in ((tiles - 1, own_group == group), (tiles, own_group != group)):
+            @pl.when(there)
+            def _():
+                part = dst.at[pl.ds(0, count)]
+                pltpu.make_async_copy(part, part, recv.at[group]).wait()
+
+    def sent_column(dst, sem):
         part = dst.at[pl.ds(0, 2 * channels - 1)]
         pltpu.make_async_copy(part, part, sem).wait()
 
@@ -375,6 +387,18 @@
         @pl.when(own_row)
         def _():
             gbuf[phase, div(r, 2)] = gtile[phase]
+        if phase == 2:
+            to_column(gtile.at[2], cbuf, col_send, col_recv)
+
+    def own_misfit():
+        collect(3)
+        mtile[0:2, :] = total[0:2, :] / (inputs - 1)
+        to_column(mtile, mbuf, mis_send, mis_recv)
+
+    def owners(group, task, *args):
+        @pl.when(own_group == group)
+        def _():
+            task(*args)
 
     def take_gains(phase, ch):
         @pl.when(jnp.logical_not(jnp.logical_and(own_row, ch == c)))
@@ -386,28 +410,75 @@
                 line = gbuf[phase, ch, 2 * comp + j : 2 * comp + j + 1, :]
                 spread[ch, comp, j * lanes : (j + 1) * lanes, :] = jnp.broadcast_to(line, (lanes, lanes)).T
 
-    lax.fori_loop(0, channels, first, 0)
-    own_gains(0)
-    for phase in (1, 2):
-        def again(ch, _):
+    def each(group, task):
+        def body(i, _):
+            task(group * per_group + i)
+            return 0
+
+        lax.fori_loop(0, per_group, body, 0)
+
+    def first(ch):
+        correlate(ch)
+        normal_sums(0, ch)
+
+    def again(phase):
+        def task(ch):
             take_gains(phase - 1, ch)
             normal_sums(phase, ch)
-            return 0
-
-        lax.fori_loop(0, channels, again, 0)
-        own_gains(phase)
-    to_column(gtile.at[2], cbuf, col_send, col_recv)
-
-    def last(ch, _):
+        return task
+
+    def last(ch):
         take_gains(2, ch)
         misfit_sums(3, ch)
+
+    def clear(ref):
+        def body(ch, _):
+            no_diagonal(ref, ch)
+            return 0
+
+        lax.fori_loop(0, channels, body, 0)
+
+    ready = SPAN + LAG * XS
+
+    def step(n, _):
+        gather(n)
+        at = jnp.maximum(n - ready, 0)
+        inside = jnp.logical_and(n >= ready, n < ready + 2 * per_group)
+
+        @pl.when(n == 4)
+        def _():
+            load_model.wait()
+            clear(mod)
+
+        @pl.when(jnp.logical_and(inside, rem(at, 2) == 0))
+        def _():
+            correlate(div(at, 2))
+
+        @pl.when(jnp.logical_and(inside, rem(at, 2) == 1))
+        def _():
+            normal_sums(0, div(at, 2))
         return 0
 
-    wait_column(cbuf, col_recv)
-    lax.fori_loop(0, channels, last, 0)
-    collect(3)
-    mtile[0:2, :] = total[0:2, :] / (inputs - 1)
-    to_column(mtile, mbuf, mis_send, mis_recv)
+    lax.fori_loop(0, STEPS + LAG * XS, step, 0)
+
+    owners(0, own_gains, 0)
+    each(1, first)
+    each(0, again(1))
+    owners(1, own_gains, 0)
+    owners(0, own_gains, 1)
+    each(1, again(1))
+    each(0, again(2))
+    owners(1, own_gains, 1)
+    owners(0, own_gains, 2)
+    each(1, again(2))
+    clear(vis)
+    wait_column(cbuf, col_recv, 0)
+    each(0, last)
+    owners(1, own_gains, 2)
+    owners(0, own_misfit)
+    wait_column(cbuf, col_recv, 1)
+    each(1, last)
+    lax.fori_loop(0, STEPS, settle, 0)
     for ch in range(channels):
         for b in (0, 1):
             for j in range(half // lanes):
@@ -415,7 +486,8 @@
                 for comp in (0, 1):
                     gains_out[ch, comp : comp + 1, cols] = cbuf[2 * ch + b, 2 * comp + j : 2 * comp + j + 1, :]
 
-    lax.fori_loop(0, STEPS, settle, 0)
+    owners(1, own_misfit)
+
     for phase in range(4):
         part = sbuf.at[phase, pl.ds(0, 2 * channels - 1)]
         pltpu.make_async_copy(part, part, part_send.at[phase]).wait()
@@ -425,9 +497,10 @@
             def _():
                 part = gbuf.at[phase, pl.ds(0, sent)]
                 pltpu.make_async_copy(part, part, gain_send.at[phase]).wait()
-    wait_column(cbuf, col_send)
-    wait_column(mbuf, mis_send)
-    wait_column(mbuf, mis_recv)
+    sent_column(cbuf, col_send)
+    sent_column(mbuf, mis_send)
+    wait_column(mbuf, mis_recv, 0)
+    wait_column(mbuf, mis_recv, 1)
     for ch in range(channels):
         for b in (0, 1):
             for j in range(half // lanes):
@@ -472,9 +545,9 @@
             dma((3,)),
             dma((3, channels)),
             dma(()),
+            dma((2,)),
             dma(()),
-            dma(()),
-            dma(()),
+            dma((2,)),
         ],
         compiler_params=pltpu.CompilerParams(
             collective_id=0, has_side_effects=True, vmem_limit_bytes=50 * 2**20

time: 176 us -> 178 us (1.011)
  the two profiles are of different devices: /device:TPU:48 before, /device:TPU:2 now
where the time goes in v2:
time: 178 us
  Pallas kernels  175 us (98%)
  local copies, waits for them, and re-layouts  2.17 us (1%)
    pallas_call x1, Pallas kernels, per_device(): pl.pallas_call(kernel, out_shape=(jax.ShapeDtypeStruct((channels, 2, widt...  175 us

profile of v2, /device:TPU:2, one launch (start us, length us, event | category | flops | bytes accessed | tf_op | source)
XLA Modules:
  0.0 178.2 jit_solution(14845667718952981444)
XLA Ops:
  0.6 0.0 copy-start
  0.6 0.9 copy-done
  1.6 175.4 %shard_map.41 = (f32[8,2,512]{2,1,0:T(2,128)S(1)}, f32[8,512]{1,0:T(8,128)S(1)}) custom-call(bf16[8,2,32,256]{3,2,1,0:T(8,128)(2,1)S(1)} %copy-done, bf16[8,2,256,512]{3,2,1,0:T(8,128)(2,1)} %model.1), custom_call_target="tpu_custom_call" | custom-call | tf_op jit(solution)/shard_map/pallas_call | solution.py:515
  177.0 0.6 copy.6
  177.6 0.6 copy.7
Async XLA Ops:
  0.6 1.0 copy-start

commit v3 on v2

--- a/solution.py
+++ b/solution.py
@@ -17,10 +17,9 @@
 LINE = 2 * RING
 HALF = RING
 GROUPS = 2
-SUBS = 2
-SPAN = (RING // 2 + 1) * SUBS
-STEPS = GROUPS * SPAN
-LAG = 2
+SUBS = 4
+STEPS = (RING // 2 + 1) * SUBS
+LAG = 4
 ROWS = 32
 TILE = (8, 128)
 
@@ -41,7 +40,7 @@
 ):
     channels = mod.shape[0]
     samples = volts.shape[3]
-    per_chunk = channels // (GROUPS * SUBS)
+    per_chunk = channels // SUBS
     per_group = channels // GROUPS
     inputs = 4096
     r = lax.axis_index("row")
@@ -95,7 +94,7 @@
 
     def split(n):
         sub = rem(n, SUBS)
-        return div(rem(n, SPAN), SUBS), sub, div(n, SPAN) * SUBS + sub
+        return div(n, SUBS), sub, sub
 
     def chunk(slot, q):
         return buf.at[slot, pl.ds(q * per_chunk, per_chunk)]
@@ -275,7 +274,7 @@
                 )
 
             zero = jnp.zeros((8, half), F32)
-            sums = lax.fori_loop(0, height // ROWS, body, (zero, zero, zero), unroll=4)
+            sums = lax.fori_loop(0, height // ROWS, body, (zero, zero, zero), unroll=2)
             for i, value in enumerate(sums):
                 put(phase, 2 * ch + b, 2 * i, jnp.sum(value, axis=0, keepdims=True))
             hand_in(phase, 2 * ch + b)
@@ -293,7 +292,7 @@
                 ei = vis[ch, 1, rows, cols] - (ai * cr - ar * ci)
                 return acc + fold(er * er + ei * ei)
 
-            total_here = lax.fori_loop(0, height // ROWS, body, jnp.zeros((8, half), F32), unroll=4)
+            total_here = lax.fori_loop(0, height // ROWS, body, jnp.zeros((8, half), F32), unroll=2)
             put(phase, 2 * ch + b, 0, jnp.sum(total_here, axis=0, keepdims=True))
             hand_in(phase, 2 * ch + b)
 
@@ -438,47 +437,34 @@
 
         lax.fori_loop(0, channels, body, 0)
 
-    ready = SPAN + LAG * XS
-
     def step(n, _):
         gather(n)
-        at = jnp.maximum(n - ready, 0)
-        inside = jnp.logical_and(n >= ready, n < ready + 2 * per_group)
-
-        @pl.when(n == 4)
+
+        @pl.when(n == SUBS - 1)
         def _():
             load_model.wait()
             clear(mod)
-
-        @pl.when(jnp.logical_and(inside, rem(at, 2) == 0))
-        def _():
-            correlate(div(at, 2))
-
-        @pl.when(jnp.logical_and(inside, rem(at, 2) == 1))
-        def _():
-            normal_sums(0, div(at, 2))
         return 0
 
     lax.fori_loop(0, STEPS + LAG * XS, step, 0)
 
-    owners(0, own_gains, 0)
+    third = STEPS // 3
+    each(0, first)
     each(1, first)
-    each(0, again(1))
-    owners(1, own_gains, 0)
-    owners(0, own_gains, 1)
-    each(1, again(1))
-    each(0, again(2))
-    owners(1, own_gains, 1)
-    owners(0, own_gains, 2)
-    each(1, again(2))
+    for phase in (0, 1, 2):
+        owners(0, own_gains, phase)
+        owners(1, own_gains, phase)
+        lax.fori_loop(phase * third, (phase + 1) * third, settle, 0)
+        if phase < 2:
+            each(0, again(phase + 1))
+            each(1, again(phase + 1))
     clear(vis)
     wait_column(cbuf, col_recv, 0)
     each(0, last)
-    owners(1, own_gains, 2)
-    owners(0, own_misfit)
     wait_column(cbuf, col_recv, 1)
     each(1, last)
-    lax.fori_loop(0, STEPS, settle, 0)
+    owners(0, own_misfit)
+    owners(1, own_misfit)
     for ch in range(channels):
         for b in (0, 1):
             for j in range(half // lanes):
@@ -486,7 +472,6 @@
                 for comp in (0, 1):
                     gains_out[ch, comp : comp + 1, cols] = cbuf[2 * ch + b, 2 * comp + j : 2 * comp + j + 1, :]
 
-    owners(1, own_misfit)
 
     for phase in range(4):
         part = sbuf.at[phase, pl.ds(0, 2 * channels - 1)]

time: 178 us -> 163 us (0.916)
  the two profiles are of different devices: /device:TPU:2 before, /device:TPU:16 now
where the time goes in v3:
time: 163 us
  Pallas kernels  160 us (98%)
  local copies, waits for them, and re-layouts  2.17 us (1%)
    pallas_call x1, Pallas kernels, per_device(): pl.pallas_call(kernel, out_shape=(jax.ShapeDtypeStruct((channels, 2, widt...  160 us

profile of v3, /device:TPU:16, one launch (start us, length us, event | category | flops | bytes accessed | tf_op | source)
XLA Modules:
  0.0 163.0 jit_solution(5221317229765664349)
XLA Ops:
  0.6 0.0 copy-start
  0.6 0.9 copy-done
  1.6 160.2 %shard_map.41 = (f32[8,2,512]{2,1,0:T(2,128)S(1)}, f32[8,512]{1,0:T(8,128)S(1)}) custom-call(bf16[8,2,32,256]{3,2,1,0:T(8,128)(2,1)S(1)} %copy-done, bf16[8,2,256,512]{3,2,1,0:T(8,128)(2,1)} %model.1), custom_call_target="tpu_custom_call" | custom-call | tf_op jit(solution)/shard_map/pallas_call | solution.py:500
  161.8 0.6 copy.6
  162.4 0.6 copy.7
Async XLA Ops:
  0.6 1.0 copy-start
